TPU v7x, 32 devices: a whole 2x2x4 slice. The times are simulated.
32 devices in a mesh: grp: 8 (over y, x, core), dom: 4 (over z).
Axes of the slice: x: 2, y: 2, z: 4, core: 2. Of those that a mesh axis runs over, the one named last changes fastest.
Arguments:
- node_feat: bfloat16 [8192, 128], P(('grp', 'dom')), may hold values from -6 to 6
- edge_feat: bfloat16 [49152, 128], P(('grp', 'dom')), may hold values from -6 to 6
- edge_src: int32 [49152], P(('grp', 'dom')), may hold values from 0 to 287, as said below
- edge_dst: int32 [49152], P(('grp', 'dom')), may hold values from 0 to 255
- halo_send: int32 [128, 8], P(('grp', 'dom')), may hold values from 0 to 255
- halo_count: int32 [32, 4], P(('grp', 'dom')), may hold values from 0 to 8, as said below
- par_send: int32 [256, 4], P(('grp', 'dom')), may hold values from 0 to 31
- par_count: int32 [32, 8], P(('grp', 'dom')), may hold values from 1 to 4, as said below
- child_slot: int32 [8192], P(('grp', 'dom')), may hold values from 0 to 31, as said below
- pool_weight: float32 [8192], P(('grp', 'dom')), may hold values from 0.1 to 1
- parent_grad: bfloat16 [1024, 128], P(('grp', 'dom')), may hold values from -6 to 6
- edge_w1: bfloat16 [384, 128], replicated, may hold values from -0.3125 to 0.3125
- edge_b1: float32 [128], replicated, may hold values from -3 to 3
- edge_w2: bfloat16 [128, 128], replicated, may hold values from -0.5 to 0.5
- node_w1: bfloat16 [256, 128], replicated, may hold values from -0.375 to 0.375
- node_b1: float32 [128], replicated, may hold values from -3 to 3
- node_w2: bfloat16 [128, 128], replicated, may hold values from -0.5 to 0.5
Outputs:
- grad_nodes: bfloat16 [8192, 128], P(('grp', 'dom'))
- grad_edges: bfloat16 [49152, 128], P(('grp', 'dom'))
- grad_edge_w1: float32 [384, 128], replicated
- grad_edge_b1: float32 [128], replicated
- grad_edge_w2: float32 [128, 128], replicated
- grad_node_w1: float32 [256, 128], replicated
- grad_node_b1: float32 [128], replicated
- grad_node_w2: float32 [128, 128], replicated
Inputs may be any that keep to these rules, and one draw needn't show every extreme that they name: `halo_count`: entry [r, j] is how many leading rows of partition r's block j of halo_send go to the partition of dom index j in r's group: 0 to itself, 1 or more to every other; in every group some partition receives 8 rows from every other one. `edge_src`: in each partition's 1536 edges the first 128 have halo sources 256 + j * 8 + s with s below the halo_count entry of the sender of dom index j for this partition; the others have own sources below 256. `par_count`: entry [r, k] is how many leading rows of partition r's block k of par_send go to the partition of grp index k with r's dom index; for every dom index some partition receives 4 rows from every grp index. `child_slot`: node n of partition (g, d) reads row k * 4 + s of parent_in, with s below par_count of partition (k, d) for grp index g.
All inputs are finite; a program needn't handle non-finite values.
Results may differ from a plain program's by a relative error of at most 0.0095.
Values may be sent and summed in bfloat16 or wider, within the bound.
A program may use at most 64 MiB of HBM per device.

v0:
```python
import jax
import jax.numpy as jnp
from jax import lax
from jax.sharding import PartitionSpec as P


def layer_norm(values):
    average = jnp.mean(values, -1, keepdims=True)
    centred = values - average
    inverse = lax.rsqrt(jnp.mean(centred * centred, -1, keepdims=True) + 1e-05)
    return (centred * inverse, inverse)


def norm_back(grad, normed, inverse):
    first = jnp.mean(grad, -1, keepdims=True)
    second = jnp.mean(grad * normed, -1, keepdims=True)
    return inverse * (grad - first - normed * second)


def silu_slope(values):
    sigmoid = jax.nn.sigmoid(values)
    return sigmoid * (1.0 + values * (1.0 - sigmoid))


def left_product(left, right):
    return lax.dot_general(
        left, right, (((0,), (0,)), ((), ())), preferred_element_type=jnp.float32
    )


def edge_back(grad_new, edge_in, edge_pre, edge_act, edge_hat, edge_inv, edge_w1, edge_w2):
    grad_elin = norm_back(grad_new, edge_hat, edge_inv).astype(jnp.bfloat16)
    grad_ew2 = left_product(edge_act, grad_elin)
    grad_eact = jnp.dot(grad_elin, edge_w2.T, preferred_element_type=jnp.float32)
    grad_epre = (grad_eact * silu_slope(edge_pre)).astype(jnp.bfloat16)
    grad_ew1 = left_product(edge_in, grad_epre)
    grad_eb1 = jnp.sum(grad_epre.astype(jnp.float32), 0)
    grad_ein = jnp.dot(grad_epre, edge_w1.T, preferred_element_type=jnp.float32)
    return (grad_ein, grad_ew1, grad_eb1, grad_ew2)


def return_halo(halo_rows, halo_send, halo_count, own_rows):
    back = lax.all_to_all(
        halo_rows.astype(jnp.bfloat16), "dom", split_axis=0, concat_axis=0, tiled=True
    ).astype(halo_rows.dtype)
    valid = jnp.arange(back.shape[1])[None, :] < halo_count[0][:, None]
    back = jnp.where(valid[:, :, None], back, 0.0)
    width = back.shape[2]
    return (
        jnp.zeros((own_rows, width), jnp.float32)
        .at[halo_send.reshape(-1)]
        .add(back.reshape(-1, width))
    )


def local(
    node_feat,
    edge_feat,
    edge_src,
    edge_dst,
    halo_send,
    halo_count,
    par_send,
    par_count,
    child_slot,
    pool_weight,
    parent_grad,
    edge_w1,
    edge_b1,
    edge_w2,
    node_w1,
    node_b1,
    node_w2,
):
    own_rows, width = node_feat.shape
    peers, slots = halo_send.shape
    halo_valid = jnp.arange(slots)[None, :] < halo_count[0][:, None]
    outgoing = jnp.where(halo_valid[:, :, None], node_feat[halo_send], jnp.zeros((), jnp.bfloat16))
    parent_valid = jnp.arange(par_send.shape[1])[None, :] < par_count[0][:, None]
    parent_out = jnp.where(
        parent_valid[:, :, None], parent_grad[par_send], jnp.zeros((), jnp.bfloat16)
    )
    incoming = lax.all_to_all(outgoing, "dom", split_axis=0, concat_axis=0, tiled=True)
    parent_in = lax.all_to_all(parent_out, "grp", split_axis=0, concat_axis=0, tiled=True)
    extended = jnp.concatenate([node_feat, incoming.reshape(-1, width)], 0)
    edge_in = jnp.concatenate([edge_feat, extended[edge_src], extended[edge_dst]], 1)
    edge_pre = jnp.dot(edge_in, edge_w1, preferred_element_type=jnp.float32) + edge_b1
    edge_act = jax.nn.silu(edge_pre).astype(jnp.bfloat16)
    edge_hat, edge_inv = layer_norm(jnp.dot(edge_act, edge_w2, preferred_element_type=jnp.float32))
    edge_new = edge_feat.astype(jnp.float32) + edge_hat
    gathered = (
        jnp.zeros((own_rows, width), jnp.float32).at[edge_dst].add(edge_new).astype(jnp.bfloat16)
    )
    node_in = jnp.concatenate([node_feat, gathered], 1)
    node_pre = jnp.dot(node_in, node_w1, preferred_element_type=jnp.float32) + node_b1
    node_act = jax.nn.silu(node_pre).astype(jnp.bfloat16)
    node_hat, node_inv = layer_norm(jnp.dot(node_act, node_w2, preferred_element_type=jnp.float32))
    grad_out = pool_weight[:, None] * parent_in.reshape(-1, width)[child_slot].astype(jnp.float32)
    grad_lin = norm_back(grad_out, node_hat, node_inv).astype(jnp.bfloat16)
    grad_nw2 = left_product(node_act, grad_lin)
    grad_act = jnp.dot(grad_lin, node_w2.T, preferred_element_type=jnp.float32)
    grad_pre = (grad_act * silu_slope(node_pre)).astype(jnp.bfloat16)
    grad_nw1 = left_product(node_in, grad_pre)
    grad_nb1 = jnp.sum(grad_pre.astype(jnp.float32), 0)
    grad_node_in = jnp.dot(grad_pre, node_w1.T, preferred_element_type=jnp.float32)
    grad_new = grad_node_in[:, width:][edge_dst]
    grad_ein, grad_ew1, grad_eb1, grad_ew2 = edge_back(
        grad_new, edge_in, edge_pre, edge_act, edge_hat, edge_inv, edge_w1, edge_w2
    )
    ext_grad = (
        jnp.zeros((own_rows + peers * slots, width), jnp.float32)
        .at[edge_src]
        .add(grad_ein[:, width : 2 * width])
    )
    ext_grad = ext_grad.at[edge_dst].add(grad_ein[:, 2 * width :])
    returned = return_halo(
        ext_grad[own_rows:].reshape(peers, slots, width), halo_send, halo_count, own_rows
    )
    own_grad = ext_grad[:own_rows]
    grad_edges = (grad_new + grad_ein[:, :width]).astype(jnp.bfloat16)
    grad_nodes = (grad_out + grad_node_in[:, :width] + own_grad + returned).astype(jnp.bfloat16)
    summed = lax.psum((grad_ew1, grad_eb1, grad_ew2, grad_nw1, grad_nb1, grad_nw2), ("grp", "dom"))
    devices = lax.axis_size("grp") * lax.axis_size("dom")
    scaled = tuple((total / devices for total in summed))
    return (
        grad_nodes,
        grad_edges,
        scaled[0],
        scaled[1],
        scaled[2],
        scaled[3],
        scaled[4],
        scaled[5],
    )


def solution(mesh):
    in_specs = (
        P(("grp", "dom"), None),
        P(("grp", "dom"), None),
        P(("grp", "dom")),
        P(("grp", "dom")),
        P(("grp", "dom"), None),
        P(("grp", "dom"), None),
        P(("grp", "dom"), None),
        P(("grp", "dom"), None),
        P(("grp", "dom")),
        P(("grp", "dom")),
        P(("grp", "dom"), None),
        P(),
        P(),
        P(),
        P(),
        P(),
        P(),
    )
    out_specs = (P(("grp", "dom"), None), P(("grp", "dom"), None), P(), P(), P(), P(), P(), P())
    return jax.shard_map(local, mesh=mesh, in_specs=in_specs, out_specs=out_specs, check_vma=False)
```

profile of v0, /device:TPU:0, one launch (start us, length us, event | category | flops | bytes accessed | tf_op | source)
XLA Modules:
  0.0 262.6 jit_solution(1641097182136597179)
XLA Ops:
  7.2 0.8 iota_compare_fusion
  8.0 0.7 compare_select_fusion.4
  8.8 0.7 compare_select_fusion.3
  9.6 1.3 gather_fusion
  10.9 0.7 broadcast_select_fusion
  11.6 5.2 %all-to-all-start = ((bf16[8,4,128]{2,1,0:T(4,128)(2,1)}), bf16[8,4,128]{2,1,0:T(4,128)(2,1)S(1)}, u32[]{:S(2)}, u32[]{:S(2)}) async-start(bf16[8,4,128]{2,1,0:T(4,128)(2,1)} %broadcast_select_fusion), calls=%async_computation | async-start | bytes 16384 | tf_op jit(solution)/shard_map/all_to_all | solution.py:84
  16.7 0.8 reshape.151
  17.5 0.7 iota_compare_fusion.1
  18.2 0.7 compare_select_fusion.5
  18.9 0.7 compare_select_fusion.2
  19.6 0.7 compare_select_fusion
  20.3 1.1 constant_dynamic-update-slice_fusion.2
  21.4 1.4 gather_fusion.2
  22.8 0.7 bitcast_select_fusion
  23.5 4.9 %all-to-all-start.1 = ((bf16[4,8,128]{2,1,0:T(8,128)(2,1)}), bf16[4,8,128]{2,1,0:T(8,128)(2,1)S(1)}, u32[]{:S(2)}, u32[]{:S(2)}) async-start(bf16[4,8,128]{2,1,0:T(8,128)(2,1)} %bitcast_select_fusion), calls=%async_computation.1 | async-start | bytes 16384 | tf_op jit(solution)/shard_map/all_to_all | solution.py:83
  28.5 0.2 copy.38
  28.6 0.9 gather_fusion.1
  29.5 0.1 copy.37
  29.6 4.4 %all-to-all-done.1 = bf16[4,8,128]{2,1,0:T(8,128)(2,1)S(1)} async-done(((bf16[4,8,128]{2,1,0:T(8,128)(2,1)}), bf16[4,8,128]{2,1,0:T(8,128)(2,1)S(1)}, u32[]{:S(2)}, u32[]{:S(2)}) %all-to-all-start.1) | async-done | bytes 8224 | tf_op jit(solution)/shard_map/all_to_all | solution.py:83
  34.0 3.2 %gather_fusion.4 = bf16[1536,128]{1,0:T(8,128)(2,1)S(1)} fusion(bf16[288,128]{1,0:T(8,128)(2,1)S(1)} %pad_maximum_fusion.3, s32[2048]{0:T(1024)S(1)} %get-tuple-element.40), kind=kCustom, calls=%fused_computation.4 | custom fusion | bytes 792576 | tf_op jit(solution)/shard_map/gather | solution.py:86
  37.2 3.2 %gather_fusion.3 = bf16[1536,128]{1,0:T(8,128)(2,1)S(1)} fusion(bf16[288,128]{1,0:T(8,128)(2,1)S(1)} %pad_maximum_fusion.3, s32[2048]{0:T(1024)S(1)} %get-tuple-element.41), kind=kCustom, calls=%fused_computation.3 | custom fusion | bytes 792576 | tf_op jit(solution)/shard_map/gather | solution.py:86
  40.5 0.1 constant_dynamic-update-slice_fusion.1
  40.6 0.1 constant_dynamic-update-slice_fusion
  40.7 0.4 copy-done.10
  41.1 1.4 multiply_convert_fusion.1
  42.6 0.3 fusion.23
  42.9 0.1 multiply_reduce_fusion.1
  43.0 0.1 convert_add_fusion
  43.2 0.3 copy.39
  43.4 8.8 %scatter_custom_fusion = f32[256,128]{1,0:T(8,128)S(1)} fusion(s32[1536]{0:T(1024)S(1)} %get-tuple-element.27, f32[1536,128]{1,0:T(8,128)S(1)} %copy.39, f32[]{:T(128)} %constant.19.clone.1), kind=kCustom, calls=%fused_computation.45 | custom fusion | flops 196608 | bytes 131076 | tf_op jit(solution)/shard_map/scatter-add | solution.py:92
  52.3 0.2 multiply_convert_fusion.3
  52.5 0.2 fusion.24
  52.9 0.8 fusion.29
  53.7 0.2 convert_reduce_fusion.1
  53.9 0.9 fusion.8
  54.8 0.2 fusion.25
  55.0 2.6 gather_fusion.5
  57.7 0.3 reduce_sum.96
  57.9 0.3 copy.41
  58.2 0.1 multiply_reduce_fusion
  58.4 0.2 multiply_convert_fusion
  58.6 0.9 fusion.28
  59.5 0.4 convert_reduce_fusion
  59.9 0.9 copy-done.3
  60.8 1.2 fusion.27
  62.0 0.5 fusion.26
  62.5 1.4 copy-done.1
  63.9 0.8 fusion.2
  64.7 8.4 %scatter_custom_fusion.1 = f32[288,128]{1,0:T(8,128)S(1)} fusion(s32[1536]{0:T(1024)S(1)} %compare_select_fusion.2, f32[1536,384]{1,0:T(8,128)} %copy-done.1, f32[]{:T(128)} %constant.19.clone.1), kind=kCustom, calls=%fused_computation.20 | custom fusion | flops 196608 | bytes 934400 | tf_op jit(solution)/shard_map/scatter-add | solution.py:113
  73.1 9.4 %scatter_custom_fusion.2 = f32[288,128]{1,0:T(8,128)S(1)} fusion(f32[288,128]{1,0:T(8,128)S(1)} %scatter_custom_fusion.1, s32[1536]{0:T(1024)S(1)} %get-tuple-element.26, f32[1536,384]{1,0:T(8,128)} %copy-done.1), kind=kCustom, calls=%fused_computation.18 | custom fusion | flops 196608 | bytes 933888 | tf_op jit(solution)/shard_map/scatter-add | solution.py:115
  82.5 0.6 fusion.16
  83.1 0.1 copy.45
  83.3 39.8 %all-reduce = (f32[128]{0:T(128)S(1)}, f32[128]{0:T(128)S(1)}) all-reduce(f32[128]{0:T(128)S(1)} %get-tuple-element.36, f32[128]{0:T(128)S(1)} %get-tuple-element.38), channel_id=1, replica_groups=mesh['grp'=8,'dom'=4] {'grp','dom'}, use_global_device_ids=true, to_apply=%region_14.15 | all-reduce | flops 256 | bytes 2048 | tf_op jit(solution)/shard_map/psum | solution.py:122
  123.2 0.5 broadcast_multiply_fusion.11
  123.7 3.2 %all-to-all-start.2 = ((bf16[4,8,128]{2,1,0:T(8,128)(2,1)}), bf16[4,8,128]{2,1,0:T(8,128)(2,1)S(1)}, u32[]{:S(2)}, u32[]{:S(2)}) async-start(bf16[4,8,128]{2,1,0:T(8,128)(2,1)} %fusion.16), calls=%async_computation.2 | async-start | bytes 16384 | tf_op jit(solution)/shard_map/all_to_all | solution.py:43
  126.9 0.5 broadcast_multiply_fusion.10
  127.5 5.0 %all-to-all-done.2 = bf16[4,8,128]{2,1,0:T(8,128)(2,1)S(1)} async-done(((bf16[4,8,128]{2,1,0:T(8,128)(2,1)}), bf16[4,8,128]{2,1,0:T(8,128)(2,1)S(1)}, u32[]{:S(2)}, u32[]{:S(2)}) %all-to-all-start.2) | async-done | bytes 8224 | tf_op jit(solution)/shard_map/all_to_all | solution.py:43
  132.5 0.9 scatter_custom_fusion.3
  133.4 0.6 convert_element_type.57
  134.0 115.7 %all-reduce.4.cloned.1.call-done = (f32[384,128]{1,0:T(8,128)}, f32[128,128]{1,0:T(8,128)}, f32[256,128]{1,0:T(8,128)}, f32[128,128]{1,0:T(8,128)}) async-done(((f32[384,128]{1,0:T(8,128)}, f32[128,128]{1,0:T(8,128)}, f32[256,128]{1,0:T(8,128)}, f32[128,128]{1,0:T(8,128)}), (f32[384,128]{1,0:T(8,128)}, f32[128,128]{1,0:T(8,128)}, f32[256,128]{1,0:T(8,128)}, ...) | async-done | bytes 458768 | tf_op jit(solution)/shard_map/psum | solution.py:122
  249.7 1.6 broadcast_multiply_fusion
  251.3 1.5 broadcast_multiply_fusion.3
  252.8 1.5 broadcast_multiply_fusion.2
  254.2 1.6 broadcast_multiply_fusion.1
  (52 shorter events, 0.8 us)
Async XLA Ops:
  7.2 33.5 %copy-start = (bf16[384,128]{1,0:T(8,128)(2,1)S(1)}, bf16[384,128]{1,0:T(8,128)(2,1)}, u32[]{:S(2)}) copy-start(bf16[384,128]{1,0:T(8,128)(2,1)} %param.28) | copy-start | bytes 294916
  7.2 21.3 %copy-start.4 = (bf16[1536,128]{1,0:T(8,128)(2,1)S(1)}, bf16[1536,128]{1,0:T(8,128)(2,1)}, u32[]{:S(2)}) copy-start(bf16[1536,128]{1,0:T(8,128)(2,1)} %param.18) | copy-start | bytes 1179652
  11.6 12.0 %all-to-all-start = ((bf16[8,4,128]{2,1,0:T(4,128)(2,1)}), bf16[8,4,128]{2,1,0:T(4,128)(2,1)S(1)}, u32[]{:S(2)}, u32[]{:S(2)}) async-start(bf16[8,4,128]{2,1,0:T(4,128)(2,1)} %broadcast_select_fusion), calls=%async_computation | async-start | bytes 16384 | tf_op jit(solution)/shard_map/all_to_all | solution.py:84
  20.3 13.7 %copy-start.5 = (bf16[256,128]{1,0:T(8,128)(2,1)S(1)}, bf16[256,128]{1,0:T(8,128)(2,1)}, u32[]{:S(2)}) copy-start(bf16[256,128]{1,0:T(8,128)(2,1)} %param.17) | copy-start | bytes 196612
  23.5 10.5 %all-to-all-start.1 = ((bf16[4,8,128]{2,1,0:T(8,128)(2,1)}), bf16[4,8,128]{2,1,0:T(8,128)(2,1)S(1)}, u32[]{:S(2)}, u32[]{:S(2)}) async-start(bf16[4,8,128]{2,1,0:T(8,128)(2,1)} %bitcast_select_fusion), calls=%async_computation.1 | async-start | bytes 16384 | tf_op jit(solution)/shard_map/all_to_all | solution.py:83
  28.4 221.2 %all-reduce.4.cloned.1.call-start = ((), (), s32[]{:S(2)}) async-start(), calls=%async_computation.3 | async-start | bytes 917504 | tf_op jit(solution)/shard_map/psum | solution.py:122
  40.5 0.7 copy-start.10
  41.1 1.4 copy-start.2
  41.1 1.4 copy-start.8
  43.1 9.1 %copy-start.6 = (bf16[256,128]{1,0:T(8,128)(2,1)S(1)}, bf16[256,128]{1,0:T(8,128)(2,1)}, u32[]{:S(2)}) copy-start(bf16[256,128]{1,0:T(8,128)(2,1)} %param.31) | copy-start | bytes 196612
  43.1 9.1 %copy-start.11 = (f32[128]{0:T(128)S(1)}, f32[128]{0:T(128)}, u32[]{:S(2)}) copy-start(f32[128]{0:T(128)} %param.32) | copy-start | bytes 1540
  43.1 9.3 %copy-start.7 = (bf16[128,128]{1,0:T(8,128)(2,1)S(1)}, bf16[128,128]{1,0:T(8,128)(2,1)}, u32[]{:S(2)}) copy-start(bf16[128,128]{1,0:T(8,128)(2,1)} %param.33) | copy-start | bytes 98308
  43.4 9.3 %copy-start.9 = (f32[256]{0:T(256)S(1)}, f32[256]{0:T(256)}, u32[]{:S(2)}) copy-start(f32[256]{0:T(256)} %param.26) | copy-start | bytes 3076
  58.4 1.1 copy-start.12
  59.5 1.3 copy-start.3
  62.4 1.4 copy-start.1
  123.7 8.8 %all-to-all-start.2 = ((bf16[4,8,128]{2,1,0:T(8,128)(2,1)}), bf16[4,8,128]{2,1,0:T(8,128)(2,1)S(1)}, u32[]{:S(2)}, u32[]{:S(2)}) async-start(bf16[4,8,128]{2,1,0:T(8,128)(2,1)} %fusion.16), calls=%async_computation.2 | async-start | bytes 16384 | tf_op jit(solution)/shard_map/all_to_all | solution.py:43
Sparse Core Ops, SparseCore 0:
  123.3 126.3 all-reduce.3
where the time goes:
time: 264 us; the launch traced here: 263 us
  waiting for transfers between devices  125 us (47%)
  other arithmetic  43.4 us (16%)
  blocking collectives  39.8 us (15%)
  local copies, waits for them, and re-layouts  19.3 us (7%)
  between operations  14.5 us (5%)
  starting transfers between devices  13.3 us (5%)
  matrix products  7.28 us (3%)
    psum x1, waiting for transfers between devices, local(): lax.psum((grad_ew1, grad_eb1, grad_ew2, grad_nw1, grad_nb1, grad_nw2), ('...  116 us
    psum x1, blocking collectives, local(): lax.psum((grad_ew1, grad_eb1, grad_ew2, grad_nw1, grad_nb1, grad_nw2), ('...  39.8 us
    scatter-add x1, other arithmetic, local(): ext_grad = ext_grad.at[edge_dst].add(grad_ein[:, 2 * width:])  9.41 us
    scatter-add x1, other arithmetic, local(): jnp.zeros((own_rows, width), jnp.float32).at[edge_dst].add(edge_new)  8.78 us
    scatter-add x1, other arithmetic, local(): ext_grad = jnp.zeros((own_rows + peers * slots, width), jnp.float32).at[e...  8.4 us
    div x6, other arithmetic, local(): scaled = tuple((total / devices for total in summed))  7.16 us
  transfers between devices with their start and end apart: 4, of which 3 were waited for; matrix products, arithmetic and copies ran while one was open for 4% of the time, Pallas kernels for 0%

commit v1 on v0

v1 whole, which is shorter than its diff:
```python
import functools

import jax
import jax.numpy as jnp
from jax import lax
from jax.experimental import pallas as pl
from jax.experimental.pallas import tpu as pltpu
from jax.sharding import PartitionSpec as P

F32, BF16 = jnp.float32, jnp.bfloat16
HALO_EDGES = 128
CHUNK = 352
SLOT = 8


def round_up(value, step):
    return -(-value // step) * step


def dot(left, right):
    return jnp.dot(left, right, preferred_element_type=F32)


def dot_nt(left, right):
    return lax.dot_general(left, right, (((1,), (1,)), ((), ())), preferred_element_type=F32)


def dot_tn(left, right):
    return lax.dot_general(left, right, (((0,), (0,)), ((), ())), preferred_element_type=F32)


def sigmoid(values):
    return 0.5 * jnp.tanh(0.5 * values) + 0.5


def mean(values):
    return jnp.mean(values, -1, keepdims=True)


def layer_norm(values):
    centred = values - mean(values)
    inverse = lax.rsqrt(mean(centred * centred) + 1e-05)
    return centred * inverse, inverse


def spread(row):
    return jnp.concatenate(
        [
            jnp.transpose(jnp.broadcast_to(row[:, at : at + 128], (128, 128)))
            for at in range(0, row.shape[1], 128)
        ],
        0,
    )


def hot_columns(spread_index, columns):
    parts = []
    for at in range(0, columns, 128):
        wide = min(128, columns - at)
        lanes = at + lax.broadcasted_iota(jnp.int32, (spread_index.shape[0], wide), 1)
        parts.append((spread_index[:, :wide] == lanes).astype(F32).astype(BF16))
    return parts[0] if len(parts) == 1 else jnp.concatenate(parts, 1)


def hot_rows(row, rows):
    return (lax.broadcasted_iota(jnp.int32, (rows, row.shape[1]), 0) == row).astype(F32).astype(BF16)


def masked_index(send, count, stride):
    peers, slots = send.shape
    parts = []
    for peer in range(peers):
        valid = lax.broadcasted_iota(jnp.int32, (1, slots), 1) < count[:, peer : peer + 1]
        parts.append(jnp.where(valid, send[peer : peer + 1, :], -1))
        if stride > slots:
            parts.append(jnp.full((1, stride - slots), -1, jnp.int32))
    return jnp.concatenate(parts, 1)


def kernel(
    groups, domains,
    node_ref, edge_ref, src_ref, dst_ref, hsend_ref, hcount_ref, psend_ref, pcount_ref,
    child_ref, pool_ref, parent_ref, ew1_ref, eb1_ref, ew2_ref, nw1_ref, nb1_ref, nw2_ref,
    gnodes_ref, gedges_ref, gew1_ref, geb1_ref, gew2_ref, gnw1_ref, gnb1_ref, gnw2_ref,
    src_cols, dst_cols, src_rows, dst_rows, dst_hot, slope, inverse, act, hat, elin, epre,
    halo_out, halo_in, par_out, par_in, ret_out, ret_in,
    a_out, a_in, a_mid, a_all, b_out, b_in, b_mid, b_all,
    g_send, g_recv, d_send, d_recv,
):
    width = 128
    own, edges = node_ref.shape[0], edge_ref.shape[0]
    halo = domains * SLOT
    par_slots = psend_ref.shape[1]
    me_g, me_d = lax.axis_index("grp"), lax.axis_index("dom")

    barrier = pltpu.get_barrier_semaphore()
    for step in range(1, groups):
        pl.semaphore_signal(
            barrier, inc=1, device_id={"grp": lax.rem(me_g + step, groups)},
            device_id_type=pl.DeviceIdType.MESH,
        )
    for step in range(1, domains):
        pl.semaphore_signal(
            barrier, inc=1, device_id={"dom": lax.rem(me_d + step, domains)},
            device_id_type=pl.DeviceIdType.MESH,
        )

    def exchange(axis, phase, source, target):
        size, me = (groups, me_g) if axis == "grp" else (domains, me_d)
        send, recv = (g_send, g_recv) if axis == "grp" else (d_send, d_recv)
        copies = []
        for step in range(1, size):
            peer = lax.rem(me + step, size)
            copy = pltpu.make_async_remote_copy(
                src_ref=source(peer), dst_ref=target,
                send_sem=send.at[phase, step], recv_sem=recv.at[phase, step],
                device_id={axis: peer}, device_id_type=pl.DeviceIdType.MESH,
            )
            copy.start()
            copies.append(copy)
        return copies

    def arrive(copies):
        for copy in copies:
            copy.wait_recv()

    nodes = node_ref[...]
    halo_index = masked_index(hsend_ref[...], hcount_ref[...], SLOT)
    halo_hot = hot_rows(halo_index, own)
    sent = dot_tn(halo_hot, nodes)
    par_index = masked_index(psend_ref[...], pcount_ref[...], SLOT)
    par_sent = dot_tn(hot_rows(par_index, parent_ref.shape[0]), parent_ref[...])
    for peer in range(domains):
        halo_out[peer] = sent[peer * SLOT : (peer + 1) * SLOT]
    for peer in range(groups):
        par_out[peer] = par_sent[peer * SLOT : (peer + 1) * SLOT]
    halo_in[me_d] = halo_out[me_d]
    par_in[me_g] = par_out[me_g]
    pl.semaphore_wait(barrier, groups + domains - 2)
    halo_copies = exchange("dom", 0, lambda peer: halo_out.at[peer], halo_in.at[me_d])
    par_copies = exchange("grp", 0, lambda peer: par_out.at[peer], par_in.at[me_g])

    @pl.loop(0, edges // 128)
    def _(step):
        at = pl.ds(pl.multiple_of(step * 128, 128), 128)
        src, dst = src_ref[:, at], dst_ref[:, at]
        src_cols[at, :] = spread(src)
        dst_cols[at, :] = spread(dst)
        src_rows[:, at] = hot_rows(src, own)
        dst_rows[:, at] = hot_rows(dst, own)

    src_term = dot(nodes, ew1_ref[width : 2 * width]).astype(BF16)
    dst_term = dot(nodes, ew1_ref[2 * width :]).astype(BF16)
    eb1 = eb1_ref[...]

    def forward(at, src_part):
        hot = hot_columns(dst_cols[at, :], own)
        dst_hot[at, :] = hot
        pre = dot(edge_ref[at, :], ew1_ref[:width]) + dot(hot, dst_term) + src_part + eb1
        gate = sigmoid(pre)
        active = pre * gate
        slope[at, :] = gate + active * (1.0 - gate)
        active = active.astype(BF16)
        act[at, :] = active
        normed, inv = layer_norm(dot(active, ew2_ref[...]))
        hat[at, :] = normed.astype(BF16)
        inverse[at, :] = jnp.broadcast_to(inv, normed.shape)

    @pl.loop(0, (edges - HALO_EDGES) // CHUNK)
    def _(step):
        at = pl.ds(pl.multiple_of(HALO_EDGES + step * CHUNK, 32), CHUNK)
        forward(at, dot(hot_columns(src_cols[at, :], own), src_term))

    feature_sum = dot(dst_rows[...], edge_ref[...])
    pool = spread(pool_ref[...])
    child = child_ref[...]
    child = (child // par_slots) * SLOT + lax.rem(child, par_slots)
    child_hot = hot_columns(spread(child), groups * SLOT)

    first = pl.ds(0, HALO_EDGES)
    arrive(halo_copies)
    halo_rows = halo_in[...].reshape(halo, width).astype(BF16)
    halo_term = dot(halo_rows, ew1_ref[width : 2 * width]).astype(BF16)
    forward(first, dot(hot_columns(src_cols[first, :] - own, halo), halo_term))

    agg = (feature_sum + dot(dst_rows[...], hat[...])).astype(BF16)
    node_pre = dot(nodes, nw1_ref[:width]) + dot(agg, nw1_ref[width:]) + nb1_ref[...]
    gate = sigmoid(node_pre)
    node_act = node_pre * gate
    node_slope = gate + node_act * (1.0 - gate)
    node_act = node_act.astype(BF16)
    node_hat, node_inv = layer_norm(dot(node_act, nw2_ref[...]))
    arrive(par_copies)
    parents = par_in[...].reshape(groups * SLOT, width).astype(BF16)
    grad_out = pool * dot(child_hot, parents)
    grad_lin = (
        node_inv * (grad_out - mean(grad_out) - node_hat * mean(grad_out * node_hat))
    ).astype(BF16)
    grad_pre = dot_nt(grad_lin, nw2_ref[...]) * node_slope
    grad_pre = grad_pre.astype(BF16)
    grad_agg = dot_nt(grad_pre, nw1_ref[width:])
    agg_terms = jnp.concatenate([grad_agg, grad_agg - mean(grad_agg)], 1).astype(BF16)

    def backward(at):
        both = dot(dst_hot[at, :], agg_terms)
        grad_new, centred = both[:, :width], both[:, width:]
        normed = hat[at, :].astype(F32)
        lin = (inverse[at, :] * (centred - normed * mean(grad_new * normed))).astype(BF16)
        elin[at, :] = lin
        pre = (dot_nt(lin, ew2_ref[...]) * slope[at, :]).astype(BF16)
        epre[at, :] = pre
        gedges_ref[at, :] = (grad_new + dot_nt(pre, ew1_ref[:width])).astype(BF16)

    backward(first)
    halo_hot_rows = hot_rows(src_ref[:, :HALO_EDGES] - own, halo)
    halo_sum = dot(halo_hot_rows, epre[first, :]).astype(BF16)
    halo_grad = dot_nt(halo_sum, ew1_ref[width : 2 * width])
    for peer in range(domains):
        ret_out[peer] = halo_grad[peer * SLOT : (peer + 1) * SLOT]
    ret_in[me_d] = ret_out[me_d]
    ret_copies = exchange("dom", 1, lambda peer: ret_out.at[peer], ret_in.at[me_d])

    def bias_block(ref, at, row):
        rows = ref.shape[0] - at
        top = lax.broadcasted_iota(jnp.int32, (rows, width), 0) == 0
        ref[at:, :] = jnp.where(top, row, 0.0).astype(BF16)

    def scatter_start(phase, out, block, landing):
        landing[me_g] = out[pl.ds(pl.multiple_of(me_g * block, 16), block), :]
        return exchange(
            "grp", phase,
            lambda peer: out.at[pl.ds(pl.multiple_of(peer * block, 16), block)],
            landing.at[me_g],
        )

    def total(ref):
        value = ref[0].astype(F32)
        for at in range(1, ref.shape[0]):
            value = value + ref[at].astype(F32)
        return value

    def middle_start(phase, landing, mid):
        mid[me_d] = total(landing).astype(BF16)
        return exchange("dom", phase, lambda peer: mid.at[me_d], mid.at[me_d])

    def gather_start(phase, mid, block, everything):
        mine = pl.ds(pl.multiple_of(me_g * block, 16), block)
        everything[mine, :] = (total(mid) * (1.0 / (groups * domains))).astype(BF16)
        return exchange("grp", phase, lambda peer: everything.at[mine], everything.at[mine])

    a_block, b_block = a_in.shape[1], b_in.shape[1]
    a_out[:width, :] = dot_tn(nodes, grad_pre).astype(BF16)
    a_out[width : 2 * width, :] = dot_tn(agg, grad_pre).astype(BF16)
    a_out[2 * width : 3 * width, :] = dot_tn(node_act, grad_lin).astype(BF16)
    bias_block(a_out, 3 * width, jnp.sum(grad_pre.astype(F32), 0, keepdims=True))
    a1 = scatter_start(1, a_out, a_block, a_in)

    @pl.loop(0, (edges - HALO_EDGES) // CHUNK)
    def _(step):
        backward(pl.ds(pl.multiple_of(HALO_EDGES + step * CHUNK, 32), CHUNK))

    arrive(a1)
    a2 = middle_start(2, a_in, a_mid)

    src_sum = dot(src_rows[...], epre[...])
    dst_sum = dot(dst_rows[...], epre[...])
    src_half, dst_half = src_sum.astype(BF16), dst_sum.astype(BF16)
    b_out[:width, :] = dot_tn(edge_ref[...], epre[...]).astype(BF16)
    b_out[width : 2 * width, :] = (
        dot_tn(nodes, src_half) + dot_tn(halo_rows, halo_sum)
    ).astype(BF16)
    b_out[2 * width : 3 * width, :] = dot_tn(nodes, dst_half).astype(BF16)
    b_out[3 * width : 4 * width, :] = dot_tn(act[...], elin[...]).astype(BF16)
    bias_block(b_out, 4 * width, jnp.sum(dst_sum, 0, keepdims=True))
    b1 = scatter_start(2, b_out, b_block, b_in)

    arrive(a2)
    a3 = gather_start(3, a_mid, a_block, a_all)

    grad_self = dot_nt(grad_pre, nw1_ref[:width])
    grad_ext = dot_nt(src_half, ew1_ref[width : 2 * width]) + dot_nt(dst_half, ew1_ref[2 * width :])
    arrive(ret_copies)
    returned = dot(halo_hot, ret_in[...].reshape(halo, width).astype(BF16))
    gnodes_ref[...] = (grad_out + grad_self + grad_ext + returned).astype(BF16)

    arrive(b1)
    b2 = middle_start(3, b_in, b_mid)
    arrive(a3)
    gnw1_ref[...] = a_all[: 2 * width, :].astype(F32)
    gnw2_ref[...] = a_all[2 * width : 3 * width, :].astype(F32)
    gnb1_ref[...] = a_all[3 * width : 3 * width + 16, :].astype(F32)[:1]
    arrive(b2)
    b3 = gather_start(4, b_mid, b_block, b_all)
    arrive(b3)
    gew1_ref[...] = b_all[: 3 * width, :].astype(F32)
    gew2_ref[...] = b_all[3 * width : 4 * width, :].astype(F32)
    geb1_ref[...] = b_all[4 * width : 4 * width + 16, :].astype(F32)[:1]
    for copies in (halo_copies, par_copies, ret_copies, a1, a2, a3, b1, b2, b3):
        for copy in copies:
            copy.wait_send()


def local(groups, domains, *args):
    (
        node_feat, edge_feat, edge_src, edge_dst, halo_send, halo_count, par_send, par_count,
        child_slot, pool_weight, parent_grad, edge_w1, edge_b1, edge_w2, node_w1, node_b1, node_w2,
    ) = args
    own, width = node_feat.shape
    edges = edge_feat.shape[0]
    a_block = round_up(-(-(3 * width + 16) // groups), 16)
    b_block = round_up(-(-(4 * width + 16) // groups), 16)
    vmem = pltpu.VMEM
    scratch = [
        vmem((edges, width), jnp.int32),
        vmem((edges, width), jnp.int32),
        vmem((own, edges), BF16),
        vmem((own, edges), BF16),
        vmem((edges, own), BF16),
        vmem((edges, width), F32),
        vmem((edges, width), F32),
        vmem((edges, width), BF16),
        vmem((edges, width), BF16),
        vmem((edges, width), BF16),
        vmem((edges, width), BF16),
        vmem((domains, SLOT, width), F32),
        vmem((domains, SLOT, width), F32),
        vmem((groups, SLOT, width), F32),
        vmem((groups, SLOT, width), F32),
        vmem((domains, SLOT, width), F32),
        vmem((domains, SLOT, width), F32),
    ]
    for block in (a_block, b_block):
        scratch += [
            vmem((groups * block, width), BF16),
            vmem((groups, block, width), BF16),
            vmem((domains, block, width), BF16),
            vmem((groups * block, width), BF16),
        ]
    scratch += [
        pltpu.SemaphoreType.DMA((5, groups)),
        pltpu.SemaphoreType.DMA((5, groups)),
        pltpu.SemaphoreType.DMA((4, domains)),
        pltpu.SemaphoreType.DMA((4, domains)),
    ]
    shape = jax.ShapeDtypeStruct
    outs = pl.pallas_call(
        functools.partial(kernel, groups, domains),
        out_shape=(
            shape((own, width), BF16),
            shape((edges, width), BF16),
            shape((3 * width, width), F32),
            shape((1, width), F32),
            shape((width, width), F32),
            shape((2 * width, width), F32),
            shape((1, width), F32),
            shape((width, width), F32),
        ),
        in_specs=[pl.BlockSpec(memory_space=vmem)] * 17,
        out_specs=(pl.BlockSpec(memory_space=vmem),) * 8,
        scratch_shapes=scratch,
        compiler_params=pltpu.CompilerParams(
            collective_id=0, has_side_effects=True, vmem_limit_bytes=40 * 1024 * 1024
        ),
        name="message_layer_grad",
    )(
        node_feat, edge_feat, edge_src[None, :], edge_dst[None, :], halo_send, halo_count,
        par_send, par_count, child_slot[None, :], pool_weight[None, :], parent_grad,
        edge_w1, edge_b1[None, :], edge_w2, node_w1, node_b1[None, :], node_w2,
    )
    return (
        outs[0], outs[1], outs[2], outs[3].reshape(width), outs[4],
        outs[5], outs[6].reshape(width), outs[7],
    )


def solution(mesh):
    rows, flat = P(("grp", "dom"), None), P(("grp", "dom"))
    in_specs = (
        rows, rows, flat, flat, rows, rows, rows, rows, flat, flat, rows,
        P(), P(), P(), P(), P(), P(),
    )
    out_specs = (rows, rows, P(), P(), P(), P(), P(), P())
    return jax.shard_map(
        functools.partial(local, mesh.shape["grp"], mesh.shape["dom"]),
        mesh=mesh, in_specs=in_specs, out_specs=out_specs, check_vma=False,
    )
```

time: 264 us -> 45 us (0.17)
  waiting for transfers between devices: 125 us -> 0 us
  other arithmetic: 43.4 us -> 0 us
  blocking collectives: 39.8 us -> 0 us
  Pallas kernels: 0 us -> 28.9 us
  between operations: 14.5 us -> 0.7 us
  starting transfers between devices: 13.3 us -> 0 us
  matrix products: 7.28 us -> 0 us
  local copies, waits for them, and re-layouts: 19.3 us -> 14.8 us
    psum x1 -> x0, waiting for transfers between devices: 116 us -> none  [local(): lax.psum((grad_ew1, grad_eb1, grad_ew2, grad_nw1, grad_nb1, grad_nw2), ('...]
    psum x1 -> x0, blocking collectives: 39.8 us -> none  [local(): lax.psum((grad_ew1, grad_eb1, grad_ew2, grad_nw1, grad_nb1, grad_nw2), ('...]
    pallas_call x0 -> x1, Pallas kernels: none -> 28.9 us  [local(): pl.pallas_call(functools.partial(kernel, groups, domains), out_shape=(sha...]
    scatter-add x4 -> x0, other arithmetic: 27.5 us -> none  [the longest x1 9.41 us: local(): ext_grad = ext_grad.at[edge_dst].add(grad_ein[:, 2 * width:])]
    all_to_all x3 -> x0, starting transfers between devices: 13.3 us -> none  [the longest x1 5.17 us: local(): lax.all_to_all(parent_out, 'grp', split_axis=0, concat_axis=0, tiled=True)]
    gather x8 -> x0, local copies, waits for them, and re-layouts: 12.9 us -> none  [the longest x1 3.21 us: local(): extended[edge_src]]
    all_to_all x3 -> x0, waiting for transfers between devices: 9.37 us -> none  [the longest x1 4.95 us: return_halo(): lax.all_to_all(halo_rows.astype(jnp.bfloat16), 'dom', split_axis=0, conca...]
    unnamed x31 -> x37, local copies, waits for them, and re-layouts: 4.32 us -> 13.4 us
  transfers between devices with their start and end apart: 4 -> 0, of which waited for: 3 -> 0; matrix products, arithmetic and copies ran while one was open for 4% -> 0% of each run, Pallas kernels for 0% -> 0%
where the time goes in v1:
time: 45 us; the launch traced here: 44.5 us
  Pallas kernels  28.9 us (64%)
  local copies, waits for them, and re-layouts  14.8 us (33%)
  between operations  0.7 us (2%)
    pallas_call x1, Pallas kernels, local(): pl.pallas_call(functools.partial(kernel, groups, domains), out_shape=(sha...  28.9 us
    unnamed x37, local copies, waits for them, and re-layouts  13.4 us

profile of v1, /device:TPU:0, one launch (start us, length us, event | category | flops | bytes accessed | tf_op | source)
XLA Modules:
  0.0 44.5 jit_solution(13713049559676728197)
XLA Ops:
  0.6 0.0 copy-start.4
  0.6 0.8 %copy.25.psend_ref = s32[8,4]{1,0:T(8,128)S(1)} copy(s32[8,4]{0,1:T(4,128)} %param.23) | data formatting | bytes 256 | tf_op args[6]
  1.4 0.7 %broadcast_in_dim.18.src_ref = s32[1,1536]{1,0:T(1,128)S(1)} reshape(s32[1536]{0:T(1024)} %param.19) | data formatting | bytes 12288 | tf_op jit(solution)/shard_map/broadcast_in_dim | solution.py:366
  2.1 0.0 copy-start.6
  2.1 0.0 copy-start.8
  2.1 0.0 copy-start.10
  2.1 0.7 %broadcast_in_dim.19.dst_ref = s32[1,1536]{1,0:T(1,128)S(1)} reshape(s32[1536]{0:T(1024)} %param.20) | data formatting | bytes 12288 | tf_op jit(solution)/shard_map/broadcast_in_dim | solution.py:366
  2.9 0.0 copy-done.4
  2.9 0.0 copy-done.6
  2.9 0.0 copy-done.8
  2.9 0.0 copy-done.10
  2.9 0.0 copy-start
  2.9 1.0 %copy-done = bf16[1536,128]{1,0:T(8,128)(2,1)S(1)} copy-done((bf16[1536,128]{1,0:T(8,128)(2,1)S(1)}, bf16[1536,128]{1,0:T(8,128)(2,1)}, u32[]{:S(2)}) %copy-start) | copy-done | bytes 393240
  3.9 0.0 copy-start.1
  3.9 0.9 %copy-done.1 = bf16[384,128]{1,0:T(8,128)(2,1)S(1)} copy-done((bf16[384,128]{1,0:T(8,128)(2,1)S(1)}, bf16[384,128]{1,0:T(8,128)(2,1)}, u32[]{:S(2)}) %copy-start.1) | copy-done | bytes 98328
  4.8 0.0 copy-start.2
  4.8 0.8 %copy-done.2 = bf16[256,128]{1,0:T(8,128)(2,1)S(1)} copy-done((bf16[256,128]{1,0:T(8,128)(2,1)S(1)}, bf16[256,128]{1,0:T(8,128)(2,1)}, u32[]{:S(2)}) %copy-start.2) | copy-done | bytes 65560
  5.6 0.0 copy-start.3
  5.6 0.8 %copy-done.3 = bf16[256,128]{1,0:T(8,128)(2,1)S(1)} copy-done((bf16[256,128]{1,0:T(8,128)(2,1)S(1)}, bf16[256,128]{1,0:T(8,128)(2,1)}, u32[]{:S(2)}) %copy-start.3) | copy-done | bytes 65560
  6.5 0.0 copy-start.5
  6.5 0.8 %copy-done.5 = bf16[128,128]{1,0:T(8,128)(2,1)S(1)} copy-done((bf16[128,128]{1,0:T(8,128)(2,1)S(1)}, bf16[128,128]{1,0:T(8,128)(2,1)}, u32[]{:S(2)}) %copy-start.5) | copy-done | bytes 32792
  7.2 0.0 copy-start.7
  7.2 0.7 %copy-done.7 = s32[4,8]{1,0:T(4,128)S(1)} copy-done((s32[4,8]{1,0:T(4,128)S(1)}, s32[4,8]{1,0:T(4,128)}, u32[]{:S(2)}) %copy-start.7) | copy-done | bytes 152
  7.9 0.0 copy-start.9
  7.9 0.7 %copy-done.9 = f32[256]{0:T(256)S(1)} copy-done((f32[256]{0:T(256)S(1)}, f32[256]{0:T(256)}, u32[]{:S(2)}) %copy-start.9) | copy-done | bytes 1048
  8.6 0.0 copy-start.11
  8.6 0.7 %copy-done.11 = s32[1,8]{1,0:T(1,128)S(1)} copy-done((s32[1,8]{1,0:T(1,128)S(1)}, s32[1,8]{1,0:T(1,128)}, u32[]{:S(2)}) %copy-start.11) | copy-done | bytes 56
  9.2 0.0 copy-start.12
  9.2 0.7 %copy-done.12 = f32[128]{0:T(128)S(1)} copy-done((f32[128]{0:T(128)S(1)}, f32[128]{0:T(128)}, u32[]{:S(2)}) %copy-start.12) | copy-done | bytes 536
  9.9 0.0 copy-start.13
  9.9 0.7 %copy-done.13 = f32[128]{0:T(128)S(1)} copy-done((f32[128]{0:T(128)S(1)}, f32[128]{0:T(128)}, u32[]{:S(2)}) %copy-start.13) | copy-done | bytes 536
  10.5 28.9 %message_layer_grad.1 = (bf16[256,128]{1,0:T(8,128)(2,1)S(1)}, bf16[1536,128]{1,0:T(8,128)(2,1)S(1)}, f32[384,128]{1,0:T(8,128)S(1)}, f32[1,128]{1,0:T(1,128)S(1...) custom-call(bf16[256,128]{1,0:T(8,128)(2,1)S(1)} %copy-done.2, ...), custom_call_target="tpu_custom_call" | custom-call | tf_op jit(solution)/shard_map/message_layer_grad/pallas_call | solution.py:346
  39.5 0.6 %copy.34 = bf16[256,128]{1,0:T(8,128)(2,1)} copy(bf16[256,128]{1,0:T(8,128)(2,1)S(1)} %get-tuple-element.32) | data formatting | bytes 131072
  40.1 0.7 %copy.35 = bf16[1536,128]{1,0:T(8,128)(2,1)} copy(bf16[1536,128]{1,0:T(8,128)(2,1)S(1)} %get-tuple-element.33) | data formatting | bytes 786432
  40.9 0.7 %copy.36 = f32[384,128]{1,0:T(8,128)} copy(f32[384,128]{1,0:T(8,128)S(1)} %get-tuple-element.34) | data formatting | bytes 393216
  41.5 0.5 %copy.37 = f32[128]{0:T(128)} copy(f32[128]{0:T(128)S(1)} %bitcast.11) | data formatting | bytes 1024
  42.0 0.6 %copy.38 = f32[128,128]{1,0:T(8,128)} copy(f32[128,128]{1,0:T(8,128)S(1)} %get-tuple-element.36) | data formatting | bytes 131072
  42.7 0.7 %copy.39 = f32[256,128]{1,0:T(8,128)} copy(f32[256,128]{1,0:T(8,128)S(1)} %get-tuple-element.37) | data formatting | bytes 262144
  43.3 0.5 %copy.40 = f32[128]{0:T(128)} copy(f32[128]{0:T(128)S(1)} %bitcast.10) | data formatting | bytes 1024
  43.8 0.6 %copy.41 = f32[128,128]{1,0:T(8,128)} copy(f32[128,128]{1,0:T(8,128)S(1)} %get-tuple-element.39) | data formatting | bytes 131072
Async XLA Ops:
  0.6 2.2 %copy-start.4 = (bf16[128,128]{1,0:T(8,128)(2,1)S(1)}, bf16[128,128]{1,0:T(8,128)(2,1)}, u32[]{:S(2)}) copy-start(bf16[128,128]{1,0:T(8,128)(2,1)} %ew2_ref.1) | copy-start | bytes 98308
  2.1 0.8 %copy-start.6 = (bf16[32,128]{1,0:T(8,128)(2,1)S(1)}, bf16[32,128]{1,0:T(8,128)(2,1)}, u32[]{:S(2)}) copy-start(bf16[32,128]{1,0:T(8,128)(2,1)} %parent_ref.1) | copy-start | bytes 24580
  2.1 0.8 %copy-start.8 = (s32[256]{0:T(256)S(1)}, s32[256]{0:T(256)}, u32[]{:S(2)}) copy-start(s32[256]{0:T(256)} %param.25) | copy-start | bytes 3076
  2.1 0.8 %copy-start.10 = (s32[1,4]{1,0:T(1,128)S(1)}, s32[1,4]{1,0:T(1,128)}, u32[]{:S(2)}) copy-start(s32[1,4]{1,0:T(1,128)} %hcount_ref.1) | copy-start | bytes 52
  2.9 1.0 %copy-start = (bf16[1536,128]{1,0:T(8,128)(2,1)S(1)}, bf16[1536,128]{1,0:T(8,128)(2,1)}, u32[]{:S(2)}) copy-start(bf16[1536,128]{1,0:T(8,128)(2,1)} %edge_ref.1) | copy-start | bytes 1179652
  3.9 0.9 %copy-start.1 = (bf16[384,128]{1,0:T(8,128)(2,1)S(1)}, bf16[384,128]{1,0:T(8,128)(2,1)}, u32[]{:S(2)}) copy-start(bf16[384,128]{1,0:T(8,128)(2,1)} %ew1_ref.1) | copy-start | bytes 294916
  4.8 0.8 %copy-start.2 = (bf16[256,128]{1,0:T(8,128)(2,1)S(1)}, bf16[256,128]{1,0:T(8,128)(2,1)}, u32[]{:S(2)}) copy-start(bf16[256,128]{1,0:T(8,128)(2,1)} %node_ref.1) | copy-start | bytes 196612
  5.6 0.8 %copy-start.3 = (bf16[256,128]{1,0:T(8,128)(2,1)S(1)}, bf16[256,128]{1,0:T(8,128)(2,1)}, u32[]{:S(2)}) copy-start(bf16[256,128]{1,0:T(8,128)(2,1)} %nw1_ref.1) | copy-start | bytes 196612
  6.5 0.8 %copy-start.5 = (bf16[128,128]{1,0:T(8,128)(2,1)S(1)}, bf16[128,128]{1,0:T(8,128)(2,1)}, u32[]{:S(2)}) copy-start(bf16[128,128]{1,0:T(8,128)(2,1)} %nw2_ref.1) | copy-start | bytes 98308
  7.2 0.7 %copy-start.7 = (s32[4,8]{1,0:T(4,128)S(1)}, s32[4,8]{1,0:T(4,128)}, u32[]{:S(2)}) copy-start(s32[4,8]{1,0:T(4,128)} %hsend_ref.1) | copy-start | bytes 388
  7.9 0.7 %copy-start.9 = (f32[256]{0:T(256)S(1)}, f32[256]{0:T(256)}, u32[]{:S(2)}) copy-start(f32[256]{0:T(256)} %param.26) | copy-start | bytes 3076
  8.6 0.7 %copy-start.11 = (s32[1,8]{1,0:T(1,128)S(1)}, s32[1,8]{1,0:T(1,128)}, u32[]{:S(2)}) copy-start(s32[1,8]{1,0:T(1,128)} %pcount_ref.1) | copy-start | bytes 100
  9.2 0.7 %copy-start.12 = (f32[128]{0:T(128)S(1)}, f32[128]{0:T(128)}, u32[]{:S(2)}) copy-start(f32[128]{0:T(128)} %param.29) | copy-start | bytes 1540
  9.9 0.7 %copy-start.13 = (f32[128]{0:T(128)S(1)}, f32[128]{0:T(128)}, u32[]{:S(2)}) copy-start(f32[128]{0:T(128)} %param.32) | copy-start | bytes 1540

commit v2 on v1

--- a/solution.py
+++ b/solution.py
@@ -9,8 +9,11 @@
 
 F32, BF16 = jnp.float32, jnp.bfloat16
 HALO_EDGES = 128
-CHUNK = 352
+CHUNK = 704
 SLOT = 8
+ARGS = 17
+LOAD_ORDER = (2, 3, 0, 4, 5, 6, 7, 10, 11, 1, 12, 13, 8, 9, 14, 15, 16)
+FIRST_LOADS = 2
 
 
 def round_up(value, step):
@@ -66,31 +69,47 @@
     return (lax.broadcasted_iota(jnp.int32, (rows, row.shape[1]), 0) == row).astype(F32).astype(BF16)
 
 
-def masked_index(send, count, stride):
+def masked_index(send, count):
     peers, slots = send.shape
     parts = []
     for peer in range(peers):
         valid = lax.broadcasted_iota(jnp.int32, (1, slots), 1) < count[:, peer : peer + 1]
         parts.append(jnp.where(valid, send[peer : peer + 1, :], -1))
-        if stride > slots:
-            parts.append(jnp.full((1, stride - slots), -1, jnp.int32))
     return jnp.concatenate(parts, 1)
 
 
 def kernel(
     groups, domains,
+    *refs,
+):
+    args, outs = refs[:ARGS], refs[ARGS : ARGS + 4]
+    local_refs, local_outs = refs[ARGS + 4 : 2 * ARGS + 4], refs[2 * ARGS + 4 : 2 * ARGS + 8]
+    load_sem, store_sem = refs[2 * ARGS + 8 : 2 * ARGS + 10]
+    loads = []
+    for at in LOAD_ORDER:
+        load = pltpu.make_async_copy(args[at], local_refs[at], load_sem.at[at])
+        load.start()
+        loads.append(load)
+    stores = [
+        pltpu.make_async_copy(local_outs[at], outs[at], store_sem.at[at]) for at in range(4)
+    ]
+    body(groups, domains, loads, stores, *local_refs, *local_outs, *refs[2 * ARGS + 10 :])
+
+
+def body(
+    groups, domains, loads, stores,
     node_ref, edge_ref, src_ref, dst_ref, hsend_ref, hcount_ref, psend_ref, pcount_ref,
     child_ref, pool_ref, parent_ref, ew1_ref, eb1_ref, ew2_ref, nw1_ref, nb1_ref, nw2_ref,
-    gnodes_ref, gedges_ref, gew1_ref, geb1_ref, gew2_ref, gnw1_ref, gnb1_ref, gnw2_ref,
+    gnodes_ref, gedges_ref, a_all, b_all,
     src_cols, dst_cols, src_rows, dst_rows, dst_hot, slope, inverse, act, hat, elin, epre,
     halo_out, halo_in, par_out, par_in, ret_out, ret_in,
-    a_out, a_in, a_mid, a_all, b_out, b_in, b_mid, b_all,
+    a_out, a_in, a_mid, b_out, b_in, b_mid,
     g_send, g_recv, d_send, d_recv,
 ):
     width = 128
     own, edges = node_ref.shape[0], edge_ref.shape[0]
     halo = domains * SLOT
-    par_slots = psend_ref.shape[1]
+    par_slots = psend_ref.shape[0]
     me_g, me_d = lax.axis_index("grp"), lax.axis_index("dom")
 
     barrier = pltpu.get_barrier_semaphore()
@@ -124,30 +143,42 @@
         for copy in copies:
             copy.wait_recv()
 
+    for load in loads[:FIRST_LOADS]:
+        load.wait()
+
+    @pl.loop(0, edges // 128, unroll=4)
+    def _(step):
+        at = pl.ds(pl.multiple_of(step * 128, 128), 128)
+        src, dst = src_ref[pl.ds(step, 1), :], dst_ref[pl.ds(step, 1), :]
+        src_cols[at, :] = spread(src)
+        dst_cols[at, :] = spread(dst)
+        src_rows[:, at] = hot_rows(src, own)
+        dst_rows[:, at] = hot_rows(dst, own)
+
+    for load in loads[FIRST_LOADS:]:
+        load.wait()
     nodes = node_ref[...]
-    halo_index = masked_index(hsend_ref[...], hcount_ref[...], SLOT)
+    halo_index = masked_index(hsend_ref[...], hcount_ref[...])
     halo_hot = hot_rows(halo_index, own)
     sent = dot_tn(halo_hot, nodes)
-    par_index = masked_index(psend_ref[...], pcount_ref[...], SLOT)
+    par_index = jnp.concatenate(
+        [
+            jnp.where(at < pcount_ref[...], psend_ref[at : at + 1, :], -1)
+            for at in range(par_slots)
+        ],
+        1,
+    )
     par_sent = dot_tn(hot_rows(par_index, parent_ref.shape[0]), parent_ref[...])
     for peer in range(domains):
         halo_out[peer] = sent[peer * SLOT : (peer + 1) * SLOT]
-    for peer in range(groups):
-        par_out[peer] = par_sent[peer * SLOT : (peer + 1) * SLOT]
+    par_out[...] = jnp.zeros_like(par_out)
+    for at in range(par_slots):
+        par_out[:, at, :] = par_sent[at * groups : (at + 1) * groups]
     halo_in[me_d] = halo_out[me_d]
     par_in[me_g] = par_out[me_g]
     pl.semaphore_wait(barrier, groups + domains - 2)
     halo_copies = exchange("dom", 0, lambda peer: halo_out.at[peer], halo_in.at[me_d])
     par_copies = exchange("grp", 0, lambda peer: par_out.at[peer], par_in.at[me_g])
-
-    @pl.loop(0, edges // 128)
-    def _(step):
-        at = pl.ds(pl.multiple_of(step * 128, 128), 128)
-        src, dst = src_ref[:, at], dst_ref[:, at]
-        src_cols[at, :] = spread(src)
-        dst_cols[at, :] = spread(dst)
-        src_rows[:, at] = hot_rows(src, own)
-        dst_rows[:, at] = hot_rows(dst, own)
 
     src_term = dot(nodes, ew1_ref[width : 2 * width]).astype(BF16)
     dst_term = dot(nodes, ew1_ref[2 * width :]).astype(BF16)
@@ -199,20 +230,18 @@
     grad_pre = dot_nt(grad_lin, nw2_ref[...]) * node_slope
     grad_pre = grad_pre.astype(BF16)
     grad_agg = dot_nt(grad_pre, nw1_ref[width:])
-    agg_terms = jnp.concatenate([grad_agg, grad_agg - mean(grad_agg)], 1).astype(BF16)
+    agg_centred = (grad_agg - mean(grad_agg)).astype(BF16)
 
     def backward(at):
-        both = dot(dst_hot[at, :], agg_terms)
-        grad_new, centred = both[:, :width], both[:, width:]
+        centred = dot(dst_hot[at, :], agg_centred)
         normed = hat[at, :].astype(F32)
-        lin = (inverse[at, :] * (centred - normed * mean(grad_new * normed))).astype(BF16)
+        lin = (inverse[at, :] * (centred - normed * mean(centred * normed))).astype(BF16)
         elin[at, :] = lin
         pre = (dot_nt(lin, ew2_ref[...]) * slope[at, :]).astype(BF16)
         epre[at, :] = pre
-        gedges_ref[at, :] = (grad_new + dot_nt(pre, ew1_ref[:width])).astype(BF16)
 
     backward(first)
-    halo_hot_rows = hot_rows(src_ref[:, :HALO_EDGES] - own, halo)
+    halo_hot_rows = hot_rows(jnp.concatenate([src_ref[at : at + 1, :] for at in range(HALO_EDGES // 128)], 1) - own, halo)
     halo_sum = dot(halo_hot_rows, epre[first, :]).astype(BF16)
     halo_grad = dot_nt(halo_sum, ew1_ref[width : 2 * width])
     for peer in range(domains):
@@ -274,6 +303,20 @@
     bias_block(b_out, 4 * width, jnp.sum(dst_sum, 0, keepdims=True))
     b1 = scatter_start(2, b_out, b_block, b_in)
 
+    grad_agg = grad_agg.astype(BF16)
+
+    def finish(at):
+        gedges_ref[at, :] = (
+            dot(dst_hot[at, :], grad_agg) + dot_nt(epre[at, :], ew1_ref[:width])
+        ).astype(BF16)
+
+    finish(first)
+
+    @pl.loop(0, (edges - HALO_EDGES) // CHUNK)
+    def _(step):
+        finish(pl.ds(pl.multiple_of(HALO_EDGES + step * CHUNK, 32), CHUNK))
+
+    stores[1].start()
     arrive(a2)
     a3 = gather_start(3, a_mid, a_block, a_all)
 
@@ -282,22 +325,58 @@
     arrive(ret_copies)
     returned = dot(halo_hot, ret_in[...].reshape(halo, width).astype(BF16))
     gnodes_ref[...] = (grad_out + grad_self + grad_ext + returned).astype(BF16)
+    stores[0].start()
 
     arrive(b1)
     b2 = middle_start(3, b_in, b_mid)
     arrive(a3)
-    gnw1_ref[...] = a_all[: 2 * width, :].astype(F32)
-    gnw2_ref[...] = a_all[2 * width : 3 * width, :].astype(F32)
-    gnb1_ref[...] = a_all[3 * width : 3 * width + 16, :].astype(F32)[:1]
+    stores[2].start()
     arrive(b2)
     b3 = gather_start(4, b_mid, b_block, b_all)
     arrive(b3)
-    gew1_ref[...] = b_all[: 3 * width, :].astype(F32)
-    gew2_ref[...] = b_all[3 * width : 4 * width, :].astype(F32)
-    geb1_ref[...] = b_all[4 * width : 4 * width + 16, :].astype(F32)[:1]
+    stores[3].start()
     for copies in (halo_copies, par_copies, ret_copies, a1, a2, a3, b1, b2, b3):
         for copy in copies:
             copy.wait_send()
+    for store in stores:
+        store.wait()
+
+
+def write_kernel(
+    nodes_ref, edges_ref, a_ref, b_ref,
+    gnodes_ref, gedges_ref, gew1_ref, geb1_ref, gew2_ref, gnw1_ref, gnb1_ref, gnw2_ref,
+    a_local, b_local, ew1, eb1, ew2, nw1, nb1, nw2, sem,
+):
+    width = 128
+    copies = []
+
+    def write(source, target):
+        copy = pltpu.make_async_copy(source, target, sem.at[len(copies)])
+        copy.start()
+        copies.append(copy)
+
+    load_a = pltpu.make_async_copy(a_ref, a_local, sem.at[8])
+    load_b = pltpu.make_async_copy(b_ref, b_local, sem.at[9])
+    load_b.start()
+    load_a.start()
+    write(edges_ref, gedges_ref)
+    write(nodes_ref, gnodes_ref)
+    load_b.wait()
+    load_a.wait()
+    ew1[...] = b_local[: 3 * width, :].astype(F32)
+    write(ew1, gew1_ref)
+    nw1[...] = a_local[: 2 * width, :].astype(F32)
+    write(nw1, gnw1_ref)
+    ew2[...] = b_local[3 * width : 4 * width, :].astype(F32)
+    write(ew2, gew2_ref)
+    nw2[...] = a_local[2 * width : 3 * width, :].astype(F32)
+    write(nw2, gnw2_ref)
+    eb1[...] = b_local[4 * width : 4 * width + 16, :].astype(F32)[:1]
+    write(eb1, geb1_ref)
+    nb1[...] = a_local[3 * width : 3 * width + 16, :].astype(F32)[:1]
+    write(nb1, gnb1_ref)
+    for copy in copies:
+        copy.wait()
 
 
 def local(groups, domains, *args):
@@ -334,7 +413,6 @@
             vmem((groups * block, width), BF16),
             vmem((groups, block, width), BF16),
             vmem((domains, block, width), BF16),
-            vmem((groups * block, width), BF16),
         ]
     scratch += [
         pltpu.SemaphoreType.DMA((5, groups)),
@@ -343,30 +421,44 @@
         pltpu.SemaphoreType.DMA((4, domains)),
     ]
     shape = jax.ShapeDtypeStruct
-    outs = pl.pallas_call(
+    operands = (
+        node_feat, edge_feat, edge_src.reshape(edges // 128, 128), edge_dst.reshape(edges // 128, 128),
+        halo_send, halo_count, par_send.T, par_count, child_slot[None, :], pool_weight[None, :],
+        parent_grad, edge_w1, edge_b1[None, :], edge_w2, node_w1, node_b1[None, :], node_w2,
+    )
+    results = (
+        shape((own, width), BF16),
+        shape((edges, width), BF16),
+        shape((groups * a_block, width), BF16),
+        shape((groups * b_block, width), BF16),
+    )
+    buffers = [vmem(array.shape, array.dtype) for array in operands + results]
+    results = pl.pallas_call(
         functools.partial(kernel, groups, domains),
-        out_shape=(
-            shape((own, width), BF16),
-            shape((edges, width), BF16),
-            shape((3 * width, width), F32),
-            shape((1, width), F32),
-            shape((width, width), F32),
-            shape((2 * width, width), F32),
-            shape((1, width), F32),
-            shape((width, width), F32),
-        ),
-        in_specs=[pl.BlockSpec(memory_space=vmem)] * 17,
-        out_specs=(pl.BlockSpec(memory_space=vmem),) * 8,
-        scratch_shapes=scratch,
+        out_shape=results,
+        in_specs=[pl.BlockSpec(memory_space=pltpu.HBM)] * ARGS,
+        out_specs=(pl.BlockSpec(memory_space=pltpu.HBM),) * 4,
+        scratch_shapes=buffers
+        + [pltpu.SemaphoreType.DMA((ARGS,)), pltpu.SemaphoreType.DMA((4,))]
+        + scratch,
         compiler_params=pltpu.CompilerParams(
-            collective_id=0, has_side_effects=True, vmem_limit_bytes=40 * 1024 * 1024
+            collective_id=0, has_side_effects=True, vmem_limit_bytes=60 * 1024 * 1024
         ),
         name="message_layer_grad",
-    )(
-        node_feat, edge_feat, edge_src[None, :], edge_dst[None, :], halo_send, halo_count,
-        par_send, par_count, child_slot[None, :], pool_weight[None, :], parent_grad,
-        edge_w1, edge_b1[None, :], edge_w2, node_w1, node_b1[None, :], node_w2,
-    )
+    )(*operands)
+    weights = [(3 * width, width), (1, width), (width, width), (2 * width, width), (1, width), (width, width)]
+    outs = pl.pallas_call(
+        write_kernel,
+        out_shape=(shape((own, width), BF16), shape((edges, width), BF16))
+        + tuple(shape(size, F32) for size in weights),
+        in_specs=[pl.BlockSpec(memory_space=pltpu.HBM)] * 4,
+        out_specs=(pl.BlockSpec(memory_space=pltpu.HBM),) * 8,
+        scratch_shapes=buffers[-2:]
+        + [vmem(size, F32) for size in weights]
+        + [pltpu.SemaphoreType.DMA((10,))],
+        compiler_params=pltpu.CompilerParams(vmem_limit_bytes=60 * 1024 * 1024),
+        name="write_results",
+    )(*results)
     return (
         outs[0], outs[1], outs[2], outs[3].reshape(width), outs[4],
         outs[5], outs[6].reshape(width), outs[7],

time: 45 us -> 45.4 us (level)
  Pallas kernels: 28.9 us -> 44.6 us
  local copies, waits for them, and re-layouts: 14.8 us -> 0 us
    pallas_call x1 -> x2, Pallas kernels: 28.9 us -> 44.6 us  [the longest x1 29.5 us: local(): pl.pallas_call(functools.partial(kernel, groups, domains), out_shape=resu...]
    unnamed x37 -> x0, local copies, waits for them, and re-layouts: 13.4 us -> none
    broadcast_in_dim x2 -> x0, local copies, waits for them, and re-layouts: 1.43 us -> none  [the longest x1 0.73 us: local(): edge_dst[None, :]]
where the time goes in v2:
time: 45.4 us; the launch traced here: 45.2 us
  Pallas kernels  44.6 us (98%)
  between operations  0.65 us (1%)
    pallas_call x1, Pallas kernels, local(): pl.pallas_call(functools.partial(kernel, groups, domains), out_shape=resu...  29.5 us
    pallas_call x1, Pallas kernels, local(): pl.pallas_call(write_kernel, out_shape=(shape((own, width), BF16), shape(...  15.1 us

profile of v2, /device:TPU:0, one launch (start us, length us, event | category | flops | bytes accessed | tf_op | source)
XLA Modules:
  0.0 45.2 jit_solution(9638806087896552750)
XLA Ops:
  0.6 29.5 %message_layer_grad.1 = (bf16[256,128]{1,0:T(8,128)(2,1)}, bf16[1536,128]{1,0:T(8,128)(2,1)}, bf16[512,128]{1,0:T(8,128)(2,1)}, bf16[640,128]{1,0:T(8,128)(2,1)}) custom-call(bf16[256,128]{1,0:T(8,128)(2,1)} %refs_0_.1, bf16[1536,128]{1,0:T(8,128)(2,1)} %refs_1_.1, s32[12,128]{1,0:T(8,128)} %bitcast.9, s32[12,128]{1,0:T(8,128)} %bitcast.10, s32[4,8]{1,0:T(4,128)} %refs_4_.1, ...), custom_call_target="tpu_custom_call" | custom-call | tf_op jit(solution)/shard_map/message_layer_grad/pallas_call | solution.py:436
  30.1 15.1 %write_results.1 = (bf16[256,128]{1,0:T(8,128)(2,1)}, bf16[1536,128]{1,0:T(8,128)(2,1)}, f32[384,128]{1,0:T(8,128)}, f32[1,128]{1,0:T(1,128)}, f32[128,128]{1,0:...) custom-call(bf16[256,128]{1,0:T(8,128)(2,1)} %get-tuple-element.20.nodes_ref, ...), custom_call_target="tpu_custom_call" | custom-call | tf_op jit(solution)/shard_map/write_results/pallas_call | solution.py:450

commit v3 on v2

--- a/solution.py
+++ b/solution.py
@@ -345,7 +345,7 @@
 def write_kernel(
     nodes_ref, edges_ref, a_ref, b_ref,
     gnodes_ref, gedges_ref, gew1_ref, geb1_ref, gew2_ref, gnw1_ref, gnb1_ref, gnw2_ref,
-    a_local, b_local, ew1, eb1, ew2, nw1, nb1, nw2, sem,
+    nodes_local, edges_local, a_local, b_local, ew1, eb1, ew2, nw1, nb1, nw2, sem,
 ):
     width = 128
     copies = []
@@ -357,10 +357,16 @@
 
     load_a = pltpu.make_async_copy(a_ref, a_local, sem.at[8])
     load_b = pltpu.make_async_copy(b_ref, b_local, sem.at[9])
+    load_nodes = pltpu.make_async_copy(nodes_ref, nodes_local, sem.at[10])
+    load_edges = pltpu.make_async_copy(edges_ref, edges_local, sem.at[11])
+    load_edges.start()
     load_b.start()
     load_a.start()
-    write(edges_ref, gedges_ref)
-    write(nodes_ref, gnodes_ref)
+    load_nodes.start()
+    load_edges.wait()
+    write(edges_local, gedges_ref)
+    load_nodes.wait()
+    write(nodes_local, gnodes_ref)
     load_b.wait()
     load_a.wait()
     ew1[...] = b_local[: 3 * width, :].astype(F32)
@@ -453,9 +459,9 @@
         + tuple(shape(size, F32) for size in weights),
         in_specs=[pl.BlockSpec(memory_space=pltpu.HBM)] * 4,
         out_specs=(pl.BlockSpec(memory_space=pltpu.HBM),) * 8,
-        scratch_shapes=buffers[-2:]
+        scratch_shapes=buffers[-4:]
         + [vmem(size, F32) for size in weights]
-        + [pltpu.SemaphoreType.DMA((10,))],
+        + [pltpu.SemaphoreType.DMA((12,))],
         compiler_params=pltpu.CompilerParams(vmem_limit_bytes=60 * 1024 * 1024),
         name="write_results",
     )(*results)

time: 45.4 us -> 32.4 us (0.71)
  Pallas kernels: 44.6 us -> 31.5 us
    pallas_call x1, Pallas kernels: 15.1 us -> 2.01 us  [local(): pl.pallas_call(write_kernel, out_shape=(shape((own, width), BF16), shape(...]
where the time goes in v3:
time: 32.4 us; the launch traced here: 32.2 us
  Pallas kernels  31.5 us (97%)
  between operations  0.65 us (2%)
    pallas_call x1, Pallas kernels, local(): pl.pallas_call(functools.partial(kernel, groups, domains), out_shape=resu...  29.5 us
    pallas_call x1, Pallas kernels, local(): pl.pallas_call(write_kernel, out_shape=(shape((own, width), BF16), shape(...  2.01 us

profile of v3, /device:TPU:0, one launch (start us, length us, event | category | flops | bytes accessed | tf_op | source)
XLA Modules:
  0.0 32.2 jit_solution(3098942638371910448)
XLA Ops:
  0.6 29.5 %message_layer_grad.1 = (bf16[256,128]{1,0:T(8,128)(2,1)}, bf16[1536,128]{1,0:T(8,128)(2,1)}, bf16[512,128]{1,0:T(8,128)(2,1)}, bf16[640,128]{1,0:T(8,128)(2,1)}) custom-call(bf16[256,128]{1,0:T(8,128)(2,1)} %refs_0_.1, bf16[1536,128]{1,0:T(8,128)(2,1)} %refs_1_.1, s32[12,128]{1,0:T(8,128)} %bitcast.9, s32[12,128]{1,0:T(8,128)} %bitcast.10, s32[4,8]{1,0:T(4,128)} %refs_4_.1, ...), custom_call_target="tpu_custom_call" | custom-call | tf_op jit(solution)/shard_map/message_layer_grad/pallas_call | solution.py:442
  30.1 2.0 %write_results.1 = (bf16[256,128]{1,0:T(8,128)(2,1)}, bf16[1536,128]{1,0:T(8,128)(2,1)}, f32[384,128]{1,0:T(8,128)}, f32[1,128]{1,0:T(1,128)}, f32[128,128]{1,0:...) custom-call(bf16[256,128]{1,0:T(8,128)(2,1)} %get-tuple-element.20.nodes_ref, ...), custom_call_target="tpu_custom_call" | custom-call | tf_op jit(solution)/shard_map/write_results/pallas_call | solution.py:456
